TPU v7x, 32 devices: a whole 2x2x4 slice. The times are simulated.
32 devices in a mesh: grp: 4 (over y, x), mem: 8 (over z, core).
Axes of the slice: x: 2, y: 2, z: 4, core: 2. Of those that a mesh axis runs over, the one named last changes fastest.
Arguments:
- solution: bfloat16 [7, 7, 7, 32, 16, 256], P(None, None, None, 'mem', 'grp'), may hold values from -1.5 to 1.5
- source: bfloat16 [7, 7, 7, 32, 16, 256], P(None, None, None, 'mem', 'grp'), may hold values from -6 to 6
- degree: int32 [32, 16, 256], P('mem', 'grp'), may hold values from 2 to 6
Outputs:
- updated: float32 [7, 7, 7, 32, 16, 256], P(None, None, None, 'mem', 'grp')
- fine_residual: bfloat16 [7, 7, 7, 32, 16, 256], P(None, None, None, 'mem', 'grp')
All inputs are finite; a program needn't handle non-finite values.
Results may differ from a plain program's by a relative error of at most 0.0049.
Values may be sent and summed in bfloat16 or wider, within the bound.
A program may use at most 128 MiB of HBM per device.

v0:
```python
import functools
import math

import jax
import jax.numpy as jnp
import numpy as np
from jax import lax
from jax.experimental import pallas as pl
from jax.experimental.pallas import tpu as pltpu
from jax.sharding import PartitionSpec as P

BF = jnp.bfloat16
F32 = jnp.float32
SCALING = 0.00390625
MESH = pl.DeviceIdType.MESH


def tables(n):
    i = np.arange(n)
    w = np.sqrt((2.0 * i + 1.0) / 2.0)
    alt = np.where(i % 2 == 0, 1.0, -1.0)
    s = i * (i + 1.0) / 2.0
    low = np.minimum(i[:, None], i[None, :]).astype(np.float64)
    even = (i[:, None] + i[None, :]) % 2 == 0
    k = np.sqrt((2.0 * i[:, None] + 1.0) * (2.0 * i[None, :] + 1.0)) / 2.0 * low * (low + 1.0) * even
    listed = (w, w * alt, w * s, -w * alt * s, k)
    return [t.astype(np.float32).astype(BF).astype(np.float64) for t in listed]


def place(lx, ly, direction):
    e = np.arange(lx * ly)
    x, y = e // ly, e % ly
    if direction == 0:
        return x, lx, ly, y
    return y, ly, 1, x


def matrices(n, lx, ly):
    right, left, rs, ls, k = tables(n)
    el = lx * ly
    eye = np.eye(el)
    out = {}
    for d in range(2):
        c, count, stride, other = place(lx, ly, d)
        g = el // count
        up = np.zeros((el, el))
        dn = np.zeros((el, el))
        hi = np.zeros((el, g))
        lo = np.zeros((el, g))
        for e in range(el):
            if c[e] < count - 1:
                up[e, e + stride] = 1.0
            else:
                hi[e, other[e]] = 1.0
            if c[e] > 0:
                dn[e, e - stride] = 1.0
            else:
                lo[e, other[e]] = 1.0
        z = np.zeros((el, g))
        for par in range(2):
            def slab(a, b, par=par):
                pad = np.zeros((el, 2 * g))
                both = np.concatenate([a, b], axis=1)
                return np.concatenate([both, pad] if par == 0 else [pad, both], axis=1)

            none = slab(z, z)
            rows = [
                [np.kron(right, eye) - np.kron(left, up), none, slab(-hi, z)],
                [0.5 * (np.kron(rs, eye) + np.kron(ls, up)), none, slab(z, 0.5 * hi)],
                [np.kron(right, dn) - np.kron(left, eye), slab(lo, z), none],
                [0.5 * (np.kron(rs, dn) + np.kron(ls, eye)), slab(z, 0.5 * lo), none],
            ]
            out[f"t{d}{par}"] = np.block(rows)
            q = np.zeros((el, el))
            rows = [
                [up, up, q, q, q, q, none, slab(hi, z)],
                [q, q, q, q, up, up, none, slab(z, hi)],
                [q, q, dn, dn, q, q, slab(lo, z), none],
                [q, q, q, q, dn, dn, slab(z, lo), none],
            ]
            out[f"s{d}{par}"] = np.block(rows)
        eh, elow = hi.T, lo.T
        zz = np.zeros((2 * g, n * el))
        u = np.concatenate([np.kron(right, eh), np.kron(rs, eh)])
        v = np.concatenate([np.kron(left, elow), np.kron(ls, elow)])
        out[f"e{d}"] = np.block([[u, zz], [zz, u], [v, zz], [zz, v]])
        zp = np.zeros((2 * g, el))
        ph = np.concatenate([eh, np.zeros((g, el))])
        plo = np.concatenate([elow, np.zeros((g, el))])
        out[f"f{d}"] = np.block([[u, zp], [zz, ph], [v, zp], [zz, plo]])
        qz = np.zeros((el, 2 * g))
        none = np.zeros((el, 4 * g))
        out[f"q{d}"] = np.block(
            [
                [up, none, np.concatenate([qz, hi, z], axis=1)],
                [dn, np.concatenate([qz, lo, z], axis=1), none],
            ]
        )
        o = np.zeros((g, el))
        cu = np.block([[o, o, eh, eh, o, o], [o, o, o, o, eh, eh]])
        cd = np.block([[elow, elow, o, o, o, o], [o, o, o, o, elow, elow]])
        cz = np.zeros_like(cu)
        out[f"c{d}"] = np.block([[cu, cz], [cz, cu], [cd, cz], [cz, cd]])
    out["tz"] = np.concatenate(
        [np.kron(right, eye), np.kron(0.5 * rs, eye), np.kron(left, eye), np.kron(0.5 * ls, eye)]
    )
    ju = -0.5 * np.kron(rs[:, None], eye)
    fu = np.kron(right[:, None], eye)
    jd = -0.5 * np.kron(ls[:, None], eye)
    fd = -np.kron(left[:, None], eye)
    out["w"] = -SCALING * np.concatenate(
        [np.kron(k, eye), ju, ju, fu, fu, jd, jd, fd, fd], axis=1
    )
    return {name: m.astype(np.float32).astype(BF) for name, m in out.items()}


def dot(a, b):
    return jnp.dot(a, b, preferred_element_type=F32)


def split(v):
    hi = v.astype(BF)
    return [hi, (v - hi.astype(F32)).astype(BF)]


def roll(v, shift):
    return pltpu.roll(v, shift % v.shape[1], 1)


def rows_of(n, d, p):
    if d == 0:
        return p, n * n
    if d == 1:
        return (p // n) * (n * n) + p % n, n
    return p * n, 1


def gather(f_ref, n, d, p):
    base, step = rows_of(n, d, p)
    return [f_ref[base + step * i] for i in range(n)]


def pair_update(n, d, field, ghosts, tmat, w, pens):
    el = field[0].shape[0]
    if d < 2:
        t = dot(tmat, jnp.concatenate(field + ghosts, axis=0))
        ju, mu, jd, md = (t[a * el : (a + 1) * el] for a in range(4))
        fu = pens[0] * ju - mu
        fd = pens[1] * jd - md
    else:
        t = dot(tmat, jnp.concatenate(field, axis=0))
        tr, gr, tl, gl = (t[a * el : (a + 1) * el] for a in range(4))
        ju = tr - roll(tl, -1)
        fu = pens[0] * ju - (gr + roll(gl, -1))
        jd = roll(ju, 1)
        fd = roll(fu, 1)
    return dot(w, jnp.concatenate(field + split(ju) + split(fu) + split(jd) + split(fd), axis=0))


def exchange_kernel(n, names, scale, sol, deg, srcc, *refs):
    count = len(names)
    mats = dict(zip(names, refs[:count]))
    (f_ref, g0lo, g0hi, g1lo, g1hi, pens, second, s_up0, s_dn0, s_up1, s_dn1, r_lo0, r_hi0, r_lo1,
     r_hi1, cs_up0, cs_dn0, cs_up1, cs_dn1, cr_lo0, cr_hi0, cr_lo1, cr_hi1, send, recv) = refs[count:]
    mem, grp = lax.axis_index("mem"), lax.axis_index("grp")
    nmem, ngrp = lax.axis_size("mem"), lax.axis_size("grp")
    below = {"grp": grp, "mem": jnp.maximum(mem - 1, 0)}
    above = {"grp": grp, "mem": jnp.minimum(mem + 1, nmem - 1)}
    south = {"grp": lax.rem(grp + ngrp - 1, ngrp), "mem": mem}
    north = {"grp": lax.rem(grp + 1, ngrp), "mem": mem}
    has_lo, has_hi = mem > 0, mem < nmem - 1
    lx, ly = sol.shape[1], sol.shape[2]
    el = lx * ly

    barrier = pltpu.get_barrier_semaphore()

    @pl.when(has_lo)
    def _():
        pl.semaphore_signal(barrier, inc=1, device_id=below, device_id_type=MESH)

    @pl.when(has_hi)
    def _():
        pl.semaphore_signal(barrier, inc=1, device_id=above, device_id_type=MESH)

    pl.semaphore_signal(barrier, inc=1, device_id=south, device_id_type=MESH)
    pl.semaphore_signal(barrier, inc=1, device_id=north, device_id_type=MESH)

    degree = deg[...]
    masks = [None] * 3 + [jnp.where(degree >= lv, 1.0, 0.0).astype(BF) for lv in range(3, n)]

    def build(i, carry):
        for j in range(n):
            for k in range(n):
                m = i * (n * n) + j * n + k
                v = jnp.concatenate([sol[m, x] for x in range(lx)], axis=0)
                mask_ref_level = max(j, k)
                f_ref[m] = v * mask_level(i, mask_ref_level)
        return carry

    def mask_level(i, lv):
        if isinstance(i, int):
            top = max(i, lv)
            return masks[top] if top > 2 else jnp.ones_like(masks[3])
        raise NotImplementedError

    for i in range(n):
        build(i, 0)

    pen = (3 * (degree + 1) * (degree + 1)).astype(F32)
    pen_b = pen.astype(BF)

    def edges(d, up, dn):
        e = mats[f"e{d}"][...]

        def body(q, carry):
            t = dot(e, jnp.concatenate(gather(f_ref, n, d, 2 * q) + gather(f_ref, n, d, 2 * q + 1), axis=0))
            up[q] = t[:el].astype(BF)
            dn[q] = t[el:].astype(BF)
            return carry

        half = (n * n) // 2
        lax.fori_loop(0, half, body, 0, unroll=4)
        t = dot(mats[f"f{d}"][...], jnp.concatenate(gather(f_ref, n, d, n * n - 1) + [pen_b], axis=0))
        up[half] = t[:el].astype(BF)
        dn[half] = t[el:].astype(BF)

    def copies(base, up0, dn0, up1, dn1, lo0, hi0, lo1, hi1):
        def mk(src, dst, k, to):
            return pltpu.make_async_remote_copy(
                src_ref=src, dst_ref=dst, send_sem=send.at[base + k], recv_sem=recv.at[base + k],
                device_id=to, device_id_type=MESH,
            )

        return (mk(up1, lo1, 2, north), mk(dn1, hi1, 3, south), mk(up0, lo0, 0, above), mk(dn0, hi0, 1, below))

    def start_y(c):
        c[0].start()
        c[1].start()

    def start_x(c, lo, hi):
        @pl.when(has_hi)
        def _():
            c[2].start()

        @pl.when(has_lo)
        def _():
            c[3].start()

        @pl.when(jnp.logical_not(has_lo))
        def _():
            lo[...] = jnp.zeros_like(lo)

        @pl.when(jnp.logical_not(has_hi))
        def _():
            hi[...] = jnp.zeros_like(hi)

    def finish(c):
        c[0].wait()
        c[1].wait()

        @pl.when(has_hi)
        def _():
            c[2].wait_send()
            c[3].wait_recv()

        @pl.when(has_lo)
        def _():
            c[3].wait_send()
            c[2].wait_recv()

    fine = copies(0, s_up0, s_dn0, s_up1, s_dn1, r_lo0, r_hi0, r_lo1, r_hi1)
    edges(1, s_up1, s_dn1)
    pl.semaphore_wait(barrier, 2 + has_lo.astype(jnp.int32) + has_hi.astype(jnp.int32))
    start_y(fine)
    edges(0, s_up0, s_dn0)
    start_x(fine, r_lo0, r_hi0)

    w_low = mats["w"][: 2 * el]
    zpen = jnp.maximum(pen, roll(pen, -1))
    pens[4] = zpen
    pens[5] = zpen
    coarse = [srcc[m].astype(F32) for m in range(8)]

    def add(d, c, t):
        a, b = c // 2, c % 2
        for i in range(2):
            m = (i * 4 + a * 2 + b, a * 4 + i * 2 + b, a * 4 + b * 2 + i)[d]
            coarse[m] = coarse[m] + t[i * el : (i + 1) * el]

    for c in range(4):
        p = (c // 2) * n + c % 2
        add(2, c, pair_update(n, 2, gather(f_ref, n, 2, p), None, mats["tz"][...], w_low, (zpen,)))

    finish(fine)
    half = (n * n) // 2
    for d, lo, hi, glo, ghi in ((0, r_lo0, r_hi0, g0lo, g0hi), (1, r_lo1, r_hi1, g1lo, g1hi)):
        glo[...] = lo[...]
        ghi[...] = hi[...]
        nb = dot(mats[f"q{d}"][...], jnp.concatenate([pen_b, lo[half], hi[half]], axis=0))
        dp = (jnp.maximum(pen, nb[:el]), jnp.maximum(pen, nb[el:]))
        pens[2 * d] = dp[0]
        pens[2 * d + 1] = dp[1]
        for c in range(4):
            p = (c // 2) * n + c % 2
            add(d, c, pair_update(n, d, gather(f_ref, n, d, p), [lo[p // 2], hi[p // 2]],
                                  mats[f"t{d}{p % 2}"][...], w_low, dp))

    first = [coarse[m] * scale[m] for m in range(8)]
    w0, w1 = math.sqrt(0.5), math.sqrt(1.5)

    def traces(d, c):
        a, b = c // 2, c % 2
        m0 = (a * 2 + b, a * 4 + b, a * 4 + b * 2)[d]
        m1 = m0 + (4, 2, 1)[d]
        v, g = w0 * first[m0], w1 * first[m1]
        return m0, m1, v + g, v - g, g

    stacked = {}
    ccop = copies(4, cs_up0, cs_dn0, cs_up1, cs_dn1, cr_lo0, cr_hi0, cr_lo1, cr_hi1)
    for d, up, dn in ((1, cs_up1, cs_dn1), (0, cs_up0, cs_dn0)):
        for c in range(4):
            _, _, tr, tl, g = traces(d, c)
            stacked[d, c] = split(tl) + split(tr) + split(g)
        for h in range(2):
            t = dot(mats[f"c{d}"][...], jnp.concatenate(stacked[d, 2 * h] + stacked[d, 2 * h + 1], axis=0))
            up[h] = t[:el].astype(BF)
            dn[h] = t[el:].astype(BF)
        if d == 1:
            start_y(ccop)
        else:
            start_x(ccop, cr_lo0, cr_hi0)

    applied = [3.0 * ((m >> 2) + ((m >> 1) & 1) + (m & 1)) * first[m] for m in range(8)]

    def lift(m0, m1, fu, fd, ju, jd):
        applied[m0] = applied[m0] + w0 * (fu - fd)
        applied[m1] = applied[m1] + w1 * ((fu + fd) - 0.5 * (ju + jd))

    for c in range(4):
        m0, m1, tr, tl, g = traces(2, c)
        ju = tr - roll(tl, -1)
        fu = 12.0 * ju - 0.5 * (g + roll(g, -1))
        lift(m0, m1, fu, roll(fu, 1), ju, roll(ju, 1))
    finish(ccop)
    for d, lo, hi in ((0, cr_lo0, cr_hi0), (1, cr_lo1, cr_hi1)):
        for c in range(4):
            m0, m1, tr, tl, g = traces(d, c)
            t = dot(mats[f"s{d}{c % 2}"][...],
                    jnp.concatenate(stacked[d, c] + [lo[c // 2], hi[c // 2]], axis=0))
            ju = tr - t[:el]
            jd = t[2 * el : 3 * el] - tl
            fu = 12.0 * ju - 0.5 * (g + t[el : 2 * el])
            fd = 12.0 * jd - 0.5 * (t[3 * el :] + g)
            lift(m0, m1, fu, fd, ju, jd)
    for m in range(8):
        second[m] = first[m] + scale[m] * (coarse[m] - SCALING * applied[m])


def fine_kernel(n, names, src, f_ref, g0lo, g0hi, g1lo, g1hi, pens, second, deg, *refs):
    count = len(names)
    mats = dict(zip(names, refs[:count]))
    updated, residual, acc, masks = refs[count:]
    lx, ly = src.shape[1], src.shape[2]
    el = lx * ly
    degree = deg[...]
    for lv in range(n):
        masks[lv] = jnp.where(degree >= lv, 1.0, 0.0)
    pairs = n * n
    w = mats["w"][...]

    def sweep(d, lo, hi):
        dp = (pens[2 * d], pens[2 * d + 1])

        def one(p, par, q):
            t = pair_update(n, d, gather(f_ref, n, d, p), [lo[q], hi[q]], mats[f"t{d}{par}"][...], w, dp)
            base, step = rows_of(n, d, p)
            for i in range(n):
                part = t[i * el : (i + 1) * el]
                if d == 0:
                    acc[base + step * i] = part
                else:
                    acc[base + step * i] += part

        def body(q, carry):
            one(2 * q, 0, q)
            one(2 * q + 1, 1, q)
            return carry

        lax.fori_loop(0, pairs // 2, body, 0, unroll=2)
        one(pairs - 1, 0, pairs // 2)

    sweep(0, g0lo, g0hi)
    sweep(1, g1lo, g1hi)
    zpen = (pens[4],)

    def body(p, carry):
        field = gather(f_ref, n, 2, p)
        t = pair_update(n, 2, field, None, mats["tz"][...], w, zpen)
        top = jnp.maximum(p // n, p % n)
        for k in range(n):
            m = p * n + k
            s = jnp.concatenate([src[m, x] for x in range(lx)], axis=0).astype(F32)
            r = masks[jnp.maximum(top, k)] * (s + acc[m] + t[k * el : (k + 1) * el])
            v = field[k].astype(F32)
            for x in range(lx):
                residual[m, x] = r[x * ly : (x + 1) * ly].astype(BF)
                updated[m, x] = v[x * ly : (x + 1) * ly]
        return carry

    lax.fori_loop(0, pairs, body, 0, unroll=2)
    for c in range(8):
        m = (c >> 2) * n * n + ((c >> 1) & 1) * n + (c & 1)
        v = f_ref[m].astype(F32) + second[c]
        for x in range(lx):
            updated[m, x] = v[x * ly : (x + 1) * ly]


def per_device(solution, source, degree):
    n = solution.shape[0]
    lx, ly, ez = solution.shape[3:]
    el, cubed, half = lx * ly, n * n * n, (n * n) // 2 + 1
    mats = matrices(n, lx, ly)
    single = [0.0 + 2.0 * 12.0 * 0.5, 3.0 + 2.0 * (12.0 * 1.5 - 1.5)]
    scale = [
        0.5 / (SCALING * (single[m >> 2] + single[(m >> 1) & 1] + single[m & 1])) for m in range(8)
    ]
    sol = solution.reshape(cubed, lx, ly, ez)
    src = source.reshape(cubed, lx, ly, ez)
    deg = degree.reshape(el, ez)
    srcc = source[:2, :2, :2].reshape(8, el, ez)
    vmem = pl.BlockSpec(memory_space=pltpu.VMEM)
    names = sorted(mats)
    sd = jax.ShapeDtypeStruct
    ghost = (half, el, ez)
    small = (2, el, ez)
    outs = pl.pallas_call(
        functools.partial(exchange_kernel, n, names, scale),
        out_shape=[sd((cubed, el, ez), BF)] + [sd(ghost, BF)] * 4 + [sd((6, el, ez), F32), sd((8, el, ez), F32)],
        in_specs=[vmem] * (3 + len(names)),
        out_specs=[vmem] * 7,
        scratch_shapes=[pltpu.VMEM(ghost, BF)] * 8 + [pltpu.VMEM(small, BF)] * 8
        + [pltpu.SemaphoreType.DMA((8,)), pltpu.SemaphoreType.DMA((8,))],
        compiler_params=pltpu.CompilerParams(
            collective_id=0, has_side_effects=True, vmem_limit_bytes=40 << 20
        ),
        name="exchange",
    )(sol, deg, srcc, *[jnp.asarray(mats[k]) for k in names])
    fnames = ["t00", "t01", "t10", "t11", "tz", "w"]
    updated, residual = pl.pallas_call(
        functools.partial(fine_kernel, n, fnames),
        out_shape=[sd((cubed, lx, ly, ez), F32), sd((cubed, lx, ly, ez), BF)],
        in_specs=[vmem] * (9 + len(fnames)),
        out_specs=[vmem] * 2,
        scratch_shapes=[pltpu.VMEM((cubed, el, ez), F32), pltpu.VMEM((n, el, ez), F32)],
        compiler_params=pltpu.CompilerParams(vmem_limit_bytes=48 << 20),
        name="fine",
    )(src, *outs, deg, *[jnp.asarray(mats[k]) for k in fnames])
    return updated.reshape(solution.shape), residual.reshape(solution.shape)


def solution(mesh):
    spec = P(None, None, None, "mem", "grp", None)
    return jax.shard_map(
        per_device,
        mesh=mesh,
        in_specs=(spec, spec, P("mem", "grp", None)),
        out_specs=(spec, spec),
        check_vma=False,
    )
```

profile of v0, /device:TPU:0, one launch (start us, length us, event | category | flops | bytes accessed | tf_op | source)
XLA Modules:
  0.0 67.9 jit_solution(11754665957789703414)
XLA Ops:
  0.6 0.0 copy-start.14
  0.6 0.0 copy-start
  0.7 0.9 %reshape.24.deg = s32[16,256]{1,0:T(8,128)S(1)} reshape(s32[4,4,256]{2,1,0:T(4,128)} %param.23) | data formatting | bytes 32768 | tf_op jit(solution)/shard_map/reshape | solution.py:429
  1.5 0.9 %slice.3 = bf16[2,2,2,4,4,256]{5,4,3,2,1,0:T(4,128)(2,1)S(1)} slice(bf16[7,7,7,4,4,256]{5,4,3,2,1,0:T(4,128)(2,1)} %param.22), slice={[0:2], [0:2], [0:2], [0:4], [0:4], [0:256]} | slice | bytes 131072 | tf_op jit(solution)/shard_map/slice | solution.py:430
  2.4 0.0 copy-start.1
  2.4 1.8 %copy-done.1 = bf16[7,7,7,4,4,256]{5,4,3,2,1,0:T(4,128)(2,1)S(1)} copy-done((bf16[7,7,7,4,4,256]{5,4,3,2,1,0:T(4,128)(2,1)S(1)}, bf16[7,7,7,4,4,256]{5,4,3,2,1,0:T(4,128)(2,1)}, u32[]{:S(2)}) %copy-start.1) | copy-done | bytes 2809880
  4.2 0.0 copy-start.3
  4.2 0.8 %copy-done.3 = bf16[112,240]{1,0:T(8,128)(2,1)S(1)} copy-done((bf16[112,240]{1,0:T(8,128)(2,1)S(1)}, bf16[112,240]{1,0:T(8,128)(2,1)}, u32[]{:S(2)}) %copy-start.3) | copy-done | bytes 53784
  5.0 0.0 copy-start.5
  5.0 0.8 %copy-done.5 = bf16[64,144]{1,0:T(8,128)(2,1)S(1)} copy-done((bf16[64,144]{1,0:T(8,128)(2,1)S(1)}, bf16[64,144]{1,0:T(8,128)(2,1)}, u32[]{:S(2)}) %copy-start.5) | copy-done | bytes 18456
  5.8 0.0 copy-start.7
  5.8 0.8 %copy-done.7 = bf16[64,144]{1,0:T(8,128)(2,1)S(1)} copy-done((bf16[64,144]{1,0:T(8,128)(2,1)S(1)}, bf16[64,144]{1,0:T(8,128)(2,1)}, u32[]{:S(2)}) %copy-start.7) | copy-done | bytes 18456
  6.6 0.0 copy-start.9
  6.6 0.8 %copy-done.9 = bf16[64,144]{1,0:T(8,128)(2,1)S(1)} copy-done((bf16[64,144]{1,0:T(8,128)(2,1)S(1)}, bf16[64,144]{1,0:T(8,128)(2,1)}, u32[]{:S(2)}) %copy-start.9) | copy-done | bytes 18456
  7.3 0.0 copy-start.11
  7.3 0.8 %copy-done.11 = bf16[64,144]{1,0:T(8,128)(2,1)S(1)} copy-done((bf16[64,144]{1,0:T(8,128)(2,1)S(1)}, bf16[64,144]{1,0:T(8,128)(2,1)}, u32[]{:S(2)}) %copy-start.11) | copy-done | bytes 18456
  8.1 0.0 copy-start.13
  8.1 0.7 %copy-done.13 = bf16[64,112]{1,0:T(8,128)(2,1)S(1)} copy-done((bf16[64,112]{1,0:T(8,128)(2,1)S(1)}, bf16[64,112]{1,0:T(8,128)(2,1)}, u32[]{:S(2)}) %copy-start.13) | copy-done | bytes 14360
  8.8 0.7 %copy-done.15 = bf16[64,128]{1,0:T(8,128)(2,1)S(1)} copy-done((bf16[64,128]{1,0:T(8,128)(2,1)S(1)}, bf16[64,128]{1,0:T(8,128)(2,1)}, u32[]{:S(2)}) %copy-start.15) | copy-done | bytes 16408
  9.5 0.0 copy-start.16
  9.5 0.7 %copy-done.16 = bf16[64,128]{1,0:T(8,128)(2,1)S(1)} copy-done((bf16[64,128]{1,0:T(8,128)(2,1)S(1)}, bf16[64,128]{1,0:T(8,128)(2,1)}, u32[]{:S(2)}) %copy-start.16) | copy-done | bytes 16408
  10.2 0.0 copy-start.17
  10.2 0.7 %copy-done.17 = bf16[64,128]{1,0:T(8,128)(2,1)S(1)} copy-done((bf16[64,128]{1,0:T(8,128)(2,1)S(1)}, bf16[64,128]{1,0:T(8,128)(2,1)}, u32[]{:S(2)}) %copy-start.17) | copy-done | bytes 16408
  10.9 0.0 copy-start.18
  10.9 0.7 %copy-done.18 = bf16[64,128]{1,0:T(8,128)(2,1)S(1)} copy-done((bf16[64,128]{1,0:T(8,128)(2,1)S(1)}, bf16[64,128]{1,0:T(8,128)(2,1)}, u32[]{:S(2)}) %copy-start.18) | copy-done | bytes 16408
  11.7 0.0 copy-start.19
  11.7 0.7 %copy-done.19 = bf16[32,224]{1,0:T(8,128)(2,1)S(1)} copy-done((bf16[32,224]{1,0:T(8,128)(2,1)S(1)}, bf16[32,224]{1,0:T(8,128)(2,1)}, u32[]{:S(2)}) %copy-start.19) | copy-done | bytes 14360
  12.4 0.0 copy-start.20
  12.4 0.7 %copy-done.20 = bf16[32,224]{1,0:T(8,128)(2,1)S(1)} copy-done((bf16[32,224]{1,0:T(8,128)(2,1)S(1)}, bf16[32,224]{1,0:T(8,128)(2,1)}, u32[]{:S(2)}) %copy-start.20) | copy-done | bytes 14360
  13.1 0.0 copy-start.21
  13.1 0.7 %copy-done.21 = bf16[32,192]{1,0:T(8,128)(2,1)S(1)} copy-done((bf16[32,192]{1,0:T(8,128)(2,1)S(1)}, bf16[32,192]{1,0:T(8,128)(2,1)}, u32[]{:S(2)}) %copy-start.21) | copy-done | bytes 12312
  13.8 0.7 %copy-done.22 = bf16[32,192]{1,0:T(8,128)(2,1)S(1)} copy-done((bf16[32,192]{1,0:T(8,128)(2,1)S(1)}, bf16[32,192]{1,0:T(8,128)(2,1)}, u32[]{:S(2)}) %copy-start.22) | copy-done | bytes 12312
  14.5 0.7 %copy-done.23 = bf16[32,48]{1,0:T(8,128)(2,1)S(1)} copy-done((bf16[32,48]{1,0:T(8,128)(2,1)S(1)}, bf16[32,48]{1,0:T(8,128)(2,1)}, u32[]{:S(2)}) %copy-start.23) | copy-done | bytes 3096
  15.2 0.7 %copy-done.24 = bf16[32,48]{1,0:T(8,128)(2,1)S(1)} copy-done((bf16[32,48]{1,0:T(8,128)(2,1)S(1)}, bf16[32,48]{1,0:T(8,128)(2,1)}, u32[]{:S(2)}) %copy-start.24) | copy-done | bytes 3096
  15.9 0.7 %copy-done.25 = bf16[32,128]{1,0:T(8,128)(2,1)S(1)} copy-done((bf16[32,128]{1,0:T(8,128)(2,1)S(1)}, bf16[32,128]{1,0:T(8,128)(2,1)}, u32[]{:S(2)}) %copy-start.25) | copy-done | bytes 8216
  16.6 0.7 %copy-done.26 = bf16[32,128]{1,0:T(8,128)(2,1)S(1)} copy-done((bf16[32,128]{1,0:T(8,128)(2,1)S(1)}, bf16[32,128]{1,0:T(8,128)(2,1)}, u32[]{:S(2)}) %copy-start.26) | copy-done | bytes 8216
  17.3 0.0 copy-start.12
  17.3 19.1 %exchange.1 = (bf16[343,16,256]{2,1,0:T(8,128)(2,1)S(1)}, bf16[25,16,256]{2,1,0:T(8,128)(2,1)S(1)}, bf16[25,16,256]{2,1,0:T(8,128)(2,1)S(1)}, bf16[25,16,256]{2,...) custom-call(bf16[343,4,4,256]{3,2,1,0:T(4,128)(2,1)S(1)} %bitcast.5, ...), custom_call_target="tpu_custom_call" | custom-call | tf_op jit(solution)/shard_map/exchange/pallas_call | solution.py:436
  36.5 0.0 copy-start.2
  36.5 1.5 %copy-done.2 = bf16[343,16,256]{2,1,0:T(8,128)(2,1)} copy-done((bf16[343,16,256]{2,1,0:T(8,128)(2,1)}, bf16[343,16,256]{2,1,0:T(8,128)(2,1)S(1)}, u32[]{:S(2)}) %copy-start.2) | copy-done | bytes 2809880
  38.0 0.0 copy-done.14
  38.0 0.0 copy-done
  38.0 0.0 copy-done.4
  38.0 0.0 copy-done.6
  38.0 0.0 copy-done.8
  38.0 0.0 copy-done.10
  38.0 0.0 copy-done.12
  38.1 29.8 %fine.1 = (f32[343,4,4,256]{3,2,1,0:T(4,128)}, bf16[343,4,4,256]{3,2,1,0:T(4,128)(2,1)}) custom-call(bf16[343,4,4,256]{3,2,1,0:T(4,128)(2,1)S(1)} %bitcast.4, bf16[343,16,256]{2,1,0:T(8,128)(2,1)} %copy-done.2, bf16[25,16,256]{2,1,0:T(8,128)(2,1)S(1)} %get-tuple-element.12.g0lo, bf16[25,16,256]{2,1,0:T(8,128)(2,1)S(1)} %get-tuple-element.13.g0hi, ...), custom_call_target="tpu_custom_call" | custom-call | tf_op jit(solution)/shard_map/fine/pallas_call | solution.py:449
  (11 shorter events, 0.0 us)
Async XLA Ops:
  0.6 37.4 %copy-start.14 = (bf16[64,112]{1,0:T(8,128)(2,1)S(1)}, bf16[64,112]{1,0:T(8,128)(2,1)}, u32[]{:S(2)}) copy-start(bf16[64,112]{1,0:T(8,128)(2,1)} %constant.52.clone.refs_16_.refs_4_) | copy-start | bytes 43012
  0.6 37.4 %copy-start = (bf16[7,7,7,4,4,256]{5,4,3,2,1,0:T(4,128)(2,1)S(1)}, bf16[7,7,7,4,4,256]{5,4,3,2,1,0:T(4,128)(2,1)}, u32[]{:S(2)}) copy-start(bf16[7,7,7,4,4,256]{5,4,3,2,1,0:T(4,128)(2,1)} %param.22) | copy-start | bytes 8429572
  2.4 1.8 %copy-start.1 = (bf16[7,7,7,4,4,256]{5,4,3,2,1,0:T(4,128)(2,1)S(1)}, bf16[7,7,7,4,4,256]{5,4,3,2,1,0:T(4,128)(2,1)}, u32[]{:S(2)}) copy-start(bf16[7,7,7,4,4,256]{5,4,3,2,1,0:T(4,128)(2,1)} %param.21) | copy-start | bytes 8429572
  4.2 0.8 %copy-start.3 = (bf16[112,240]{1,0:T(8,128)(2,1)S(1)}, bf16[112,240]{1,0:T(8,128)(2,1)}, u32[]{:S(2)}) copy-start(bf16[112,240]{1,0:T(8,128)(2,1)} %constant.53.clone.refs_17_.refs_5_) | copy-start | bytes 161284
  5.0 0.8 %copy-start.5 = (bf16[64,144]{1,0:T(8,128)(2,1)S(1)}, bf16[64,144]{1,0:T(8,128)(2,1)}, u32[]{:S(2)}) copy-start(bf16[64,144]{1,0:T(8,128)(2,1)} %constant.51.clone.refs_15_.refs_3_) | copy-start | bytes 55300
  5.8 0.8 %copy-start.7 = (bf16[64,144]{1,0:T(8,128)(2,1)S(1)}, bf16[64,144]{1,0:T(8,128)(2,1)}, u32[]{:S(2)}) copy-start(bf16[64,144]{1,0:T(8,128)(2,1)} %constant.50.clone.refs_14_.refs_2_) | copy-start | bytes 55300
  6.6 0.8 %copy-start.9 = (bf16[64,144]{1,0:T(8,128)(2,1)S(1)}, bf16[64,144]{1,0:T(8,128)(2,1)}, u32[]{:S(2)}) copy-start(bf16[64,144]{1,0:T(8,128)(2,1)} %constant.49.clone.refs_13_.refs_1_) | copy-start | bytes 55300
  7.3 0.8 %copy-start.11 = (bf16[64,144]{1,0:T(8,128)(2,1)S(1)}, bf16[64,144]{1,0:T(8,128)(2,1)}, u32[]{:S(2)}) copy-start(bf16[64,144]{1,0:T(8,128)(2,1)} %constant.48.clone.refs_12_.refs_0_) | copy-start | bytes 55300
  8.1 0.7 %copy-start.13 = (bf16[64,112]{1,0:T(8,128)(2,1)S(1)}, bf16[64,112]{1,0:T(8,128)(2,1)}, u32[]{:S(2)}) copy-start(bf16[64,112]{1,0:T(8,128)(2,1)} %constant.52.clone.refs_16_.refs_4_) | copy-start | bytes 43012
  8.8 0.7 %copy-start.15 = (bf16[64,128]{1,0:T(8,128)(2,1)S(1)}, bf16[64,128]{1,0:T(8,128)(2,1)}, u32[]{:S(2)}) copy-start(bf16[64,128]{1,0:T(8,128)(2,1)} %constant.47.clone.refs_11_) | copy-start | bytes 49156
  9.5 0.7 %copy-start.16 = (bf16[64,128]{1,0:T(8,128)(2,1)S(1)}, bf16[64,128]{1,0:T(8,128)(2,1)}, u32[]{:S(2)}) copy-start(bf16[64,128]{1,0:T(8,128)(2,1)} %constant.46.clone.refs_10_) | copy-start | bytes 49156
  10.2 0.7 %copy-start.17 = (bf16[64,128]{1,0:T(8,128)(2,1)S(1)}, bf16[64,128]{1,0:T(8,128)(2,1)}, u32[]{:S(2)}) copy-start(bf16[64,128]{1,0:T(8,128)(2,1)} %constant.45.clone.refs_9_) | copy-start | bytes 49156
  10.9 0.7 %copy-start.18 = (bf16[64,128]{1,0:T(8,128)(2,1)S(1)}, bf16[64,128]{1,0:T(8,128)(2,1)}, u32[]{:S(2)}) copy-start(bf16[64,128]{1,0:T(8,128)(2,1)} %constant.44.clone.refs_8_) | copy-start | bytes 49156
  11.7 0.7 %copy-start.19 = (bf16[32,224]{1,0:T(8,128)(2,1)S(1)}, bf16[32,224]{1,0:T(8,128)(2,1)}, u32[]{:S(2)}) copy-start(bf16[32,224]{1,0:T(8,128)(2,1)} %constant.39.clone.refs_3_) | copy-start | bytes 43012
  12.4 0.7 %copy-start.20 = (bf16[32,224]{1,0:T(8,128)(2,1)S(1)}, bf16[32,224]{1,0:T(8,128)(2,1)}, u32[]{:S(2)}) copy-start(bf16[32,224]{1,0:T(8,128)(2,1)} %constant.38.clone.refs_2_) | copy-start | bytes 43012
  13.1 0.7 %copy-start.21 = (bf16[32,192]{1,0:T(8,128)(2,1)S(1)}, bf16[32,192]{1,0:T(8,128)(2,1)}, u32[]{:S(2)}) copy-start(bf16[32,192]{1,0:T(8,128)(2,1)} %constant.37.clone.refs_1_) | copy-start | bytes 36868
  13.8 0.7 %copy-start.22 = (bf16[32,192]{1,0:T(8,128)(2,1)S(1)}, bf16[32,192]{1,0:T(8,128)(2,1)}, u32[]{:S(2)}) copy-start(bf16[32,192]{1,0:T(8,128)(2,1)} %constant.36.clone.refs_0_) | copy-start | bytes 36868
  14.5 0.7 %copy-start.23 = (bf16[32,48]{1,0:T(8,128)(2,1)S(1)}, bf16[32,48]{1,0:T(8,128)(2,1)}, u32[]{:S(2)}) copy-start(bf16[32,48]{1,0:T(8,128)(2,1)} %constant.43.clone.refs_7_) | copy-start | bytes 9220
  15.2 0.7 %copy-start.24 = (bf16[32,48]{1,0:T(8,128)(2,1)S(1)}, bf16[32,48]{1,0:T(8,128)(2,1)}, u32[]{:S(2)}) copy-start(bf16[32,48]{1,0:T(8,128)(2,1)} %constant.42.clone.refs_6_) | copy-start | bytes 9220
  15.9 0.7 %copy-start.25 = (bf16[32,128]{1,0:T(8,128)(2,1)S(1)}, bf16[32,128]{1,0:T(8,128)(2,1)}, u32[]{:S(2)}) copy-start(bf16[32,128]{1,0:T(8,128)(2,1)} %constant.41.clone.refs_5_) | copy-start | bytes 24580
  16.6 0.7 %copy-start.26 = (bf16[32,128]{1,0:T(8,128)(2,1)S(1)}, bf16[32,128]{1,0:T(8,128)(2,1)}, u32[]{:S(2)}) copy-start(bf16[32,128]{1,0:T(8,128)(2,1)} %constant.40.clone.refs_4_) | copy-start | bytes 24580
  17.3 20.7 %copy-start.4 = (bf16[112,240]{1,0:T(8,128)(2,1)S(1)}, bf16[112,240]{1,0:T(8,128)(2,1)}, u32[]{:S(2)}) copy-start(bf16[112,240]{1,0:T(8,128)(2,1)} %constant.53.clone.refs_17_.refs_5_) | copy-start | bytes 161284
  17.3 20.7 %copy-start.6 = (bf16[64,144]{1,0:T(8,128)(2,1)S(1)}, bf16[64,144]{1,0:T(8,128)(2,1)}, u32[]{:S(2)}) copy-start(bf16[64,144]{1,0:T(8,128)(2,1)} %constant.51.clone.refs_15_.refs_3_) | copy-start | bytes 55300
  17.3 20.7 %copy-start.8 = (bf16[64,144]{1,0:T(8,128)(2,1)S(1)}, bf16[64,144]{1,0:T(8,128)(2,1)}, u32[]{:S(2)}) copy-start(bf16[64,144]{1,0:T(8,128)(2,1)} %constant.50.clone.refs_14_.refs_2_) | copy-start | bytes 55300
  17.3 20.7 %copy-start.10 = (bf16[64,144]{1,0:T(8,128)(2,1)S(1)}, bf16[64,144]{1,0:T(8,128)(2,1)}, u32[]{:S(2)}) copy-start(bf16[64,144]{1,0:T(8,128)(2,1)} %constant.49.clone.refs_13_.refs_1_) | copy-start | bytes 55300
  17.3 20.7 %copy-start.12 = (bf16[64,144]{1,0:T(8,128)(2,1)S(1)}, bf16[64,144]{1,0:T(8,128)(2,1)}, u32[]{:S(2)}) copy-start(bf16[64,144]{1,0:T(8,128)(2,1)} %constant.48.clone.refs_12_.refs_0_) | copy-start | bytes 55300
  36.5 1.5 %copy-start.2 = (bf16[343,16,256]{2,1,0:T(8,128)(2,1)}, bf16[343,16,256]{2,1,0:T(8,128)(2,1)S(1)}, u32[]{:S(2)}) copy-start(bf16[343,16,256]{2,1,0:T(8,128)(2,1)S(1)} %get-tuple-element.11.f_ref) | copy-start | bytes 8429572
where the time goes:
time: 69.2 us; the launch traced here: 67.9 us
  Pallas kernels  49 us (71%)
  local copies, waits for them, and re-layouts  18.2 us (26%)
  between operations  0.74 us (1%)
    pallas_call x1, Pallas kernels, per_device(): pl.pallas_call(functools.partial(fine_kernel, n, fnames), out_shape=[sd((...  29.8 us
    pallas_call x1, Pallas kernels, per_device(): pl.pallas_call(functools.partial(exchange_kernel, n, names, scale), out_s...  19.1 us
    unnamed x54, local copies, waits for them, and re-layouts  16.4 us

commit v1 on v0

--- a/solution.py
+++ b/solution.py
@@ -140,28 +140,47 @@
     return [f_ref[base + step * i] for i in range(n)]
 
 
-def pair_update(n, d, field, ghosts, tmat, w, pens):
-    el = field[0].shape[0]
+def mean_jump(t, el):
+    return (t[a * el : (a + 1) * el] for a in range(4))
+
+
+def sweep(n, d, f_ref, pairs, ghosts, tmats, w, pens):
+    el = f_ref.shape[1]
+    fields = [gather(f_ref, n, d, p) for p in pairs]
     if d < 2:
-        t = dot(tmat, jnp.concatenate(field + ghosts, axis=0))
-        ju, mu, jd, md = (t[a * el : (a + 1) * el] for a in range(4))
-        fu = pens[0] * ju - mu
-        fd = pens[1] * jd - md
+        lo, hi = ghosts
+        firsts = [
+            dot(tmats[p % 2], jnp.concatenate(field + [lo[p // 2], hi[p // 2]], axis=0))
+            for p, field in zip(pairs, fields)
+        ]
     else:
-        t = dot(tmat, jnp.concatenate(field, axis=0))
-        tr, gr, tl, gl = (t[a * el : (a + 1) * el] for a in range(4))
-        ju = tr - roll(tl, -1)
-        fu = pens[0] * ju - (gr + roll(gl, -1))
-        jd = roll(ju, 1)
-        fd = roll(fu, 1)
-    return dot(w, jnp.concatenate(field + split(ju) + split(fu) + split(jd) + split(fd), axis=0))
-
-
-def exchange_kernel(n, names, scale, sol, deg, srcc, *refs):
-    count = len(names)
-    mats = dict(zip(names, refs[:count]))
-    (f_ref, g0lo, g0hi, g1lo, g1hi, pens, second, s_up0, s_dn0, s_up1, s_dn1, r_lo0, r_hi0, r_lo1,
-     r_hi1, cs_up0, cs_dn0, cs_up1, cs_dn1, cr_lo0, cr_hi0, cr_lo1, cr_hi1, send, recv) = refs[count:]
+        firsts = [dot(tmats[0], jnp.concatenate(field, axis=0)) for field in fields]
+    faces = []
+    for t in firsts:
+        if d < 2:
+            ju, mu, jd, md = mean_jump(t, el)
+            fu = pens[0] * ju - mu
+            fd = pens[1] * jd - md
+            faces.append(split(ju) + split(fu) + split(jd) + split(fd))
+        else:
+            tr, gr, tl, gl = mean_jump(t, el)
+            ju = tr - roll(tl, -1)
+            fu = pens[0] * ju - (gr + roll(gl, -1))
+            faces.append(split(ju) + split(fu) + split(roll(ju, 1)) + split(roll(fu, 1)))
+    return [dot(w, jnp.concatenate(field + face, axis=0)) for field, face in zip(fields, faces)]
+
+
+def batches(total, size):
+    return [list(range(a, min(a + size, total))) for a in range(0, total, size)]
+
+
+def exchange_kernel(n, slots, scale, sol, src, deg, packed, f_ref, acc, g1lo, g1hi, pens, second,
+                    s_up0, s_dn0, s_up1, s_dn1, r_lo0, r_hi0, r_lo1, r_hi1,
+                    cs_up0, cs_dn0, cs_up1, cs_dn1, cr_lo0, cr_hi0, cr_lo1, cr_hi1, send, recv):
+    def mat(name):
+        off, rows, cols = slots[name]
+        return packed[off : off + rows, :cols]
+
     mem, grp = lax.axis_index("mem"), lax.axis_index("grp")
     nmem, ngrp = lax.axis_size("mem"), lax.axis_size("grp")
     below = {"grp": grp, "mem": jnp.maximum(mem - 1, 0)}
@@ -171,6 +190,7 @@
     has_lo, has_hi = mem > 0, mem < nmem - 1
     lx, ly = sol.shape[1], sol.shape[2]
     el = lx * ly
+    cubed, pairs, half = n * n * n, n * n, (n * n) // 2
 
     barrier = pltpu.get_barrier_semaphore()
 
@@ -185,49 +205,33 @@
     pl.semaphore_signal(barrier, inc=1, device_id=south, device_id_type=MESH)
     pl.semaphore_signal(barrier, inc=1, device_id=north, device_id_type=MESH)
 
-    degree = deg[...]
-    masks = [None] * 3 + [jnp.where(degree >= lv, 1.0, 0.0).astype(BF) for lv in range(3, n)]
-
-    def build(i, carry):
-        for j in range(n):
-            for k in range(n):
-                m = i * (n * n) + j * n + k
-                v = jnp.concatenate([sol[m, x] for x in range(lx)], axis=0)
-                mask_ref_level = max(j, k)
-                f_ref[m] = v * mask_level(i, mask_ref_level)
-        return carry
-
-    def mask_level(i, lv):
-        if isinstance(i, int):
-            top = max(i, lv)
-            return masks[top] if top > 2 else jnp.ones_like(masks[3])
-        raise NotImplementedError
-
-    for i in range(n):
-        build(i, 0)
+    degree = jnp.concatenate([deg[x] for x in range(lx)], axis=0)
+    masks = {lv: jnp.where(degree >= lv, 1.0, 0.0).astype(BF) for lv in range(3, n)}
+    for m in range(cubed):
+        f_ref[m] = jnp.concatenate([sol[m, x] for x in range(lx)], axis=0)
+    for m in range(cubed):
+        top = max(m // pairs, (m // n) % n, m % n)
+        if top > 2:
+            f_ref[m] = f_ref[m] * masks[top]
 
     pen = (3 * (degree + 1) * (degree + 1)).astype(F32)
     pen_b = pen.astype(BF)
 
     def edges(d, up, dn):
-        e = mats[f"e{d}"][...]
-
-        def body(q, carry):
-            t = dot(e, jnp.concatenate(gather(f_ref, n, d, 2 * q) + gather(f_ref, n, d, 2 * q + 1), axis=0))
+        e = mat(f"e{d}")
+        out = [
+            dot(e, jnp.concatenate(gather(f_ref, n, d, 2 * q) + gather(f_ref, n, d, 2 * q + 1), axis=0))
+            for q in range(half)
+        ]
+        out.append(dot(mat(f"f{d}"), jnp.concatenate(gather(f_ref, n, d, pairs - 1) + [pen_b], axis=0)))
+        for q, t in enumerate(out):
             up[q] = t[:el].astype(BF)
             dn[q] = t[el:].astype(BF)
-            return carry
-
-        half = (n * n) // 2
-        lax.fori_loop(0, half, body, 0, unroll=4)
-        t = dot(mats[f"f{d}"][...], jnp.concatenate(gather(f_ref, n, d, n * n - 1) + [pen_b], axis=0))
-        up[half] = t[:el].astype(BF)
-        dn[half] = t[el:].astype(BF)
 
     def copies(base, up0, dn0, up1, dn1, lo0, hi0, lo1, hi1):
-        def mk(src, dst, k, to):
+        def mk(a, b, k, to):
             return pltpu.make_async_remote_copy(
-                src_ref=src, dst_ref=dst, send_sem=send.at[base + k], recv_sem=recv.at[base + k],
+                src_ref=a, dst_ref=b, send_sem=send.at[base + k], recv_sem=recv.at[base + k],
                 device_id=to, device_id_type=MESH,
             )
 
@@ -275,35 +279,37 @@
     edges(0, s_up0, s_dn0)
     start_x(fine, r_lo0, r_hi0)
 
-    w_low = mats["w"][: 2 * el]
+    w = mat("w")
+    w_low = w[: 2 * el]
     zpen = jnp.maximum(pen, roll(pen, -1))
-    pens[4] = zpen
-    pens[5] = zpen
-    coarse = [srcc[m].astype(F32) for m in range(8)]
-
-    def add(d, c, t):
-        a, b = c // 2, c % 2
-        for i in range(2):
-            m = (i * 4 + a * 2 + b, a * 4 + i * 2 + b, a * 4 + b * 2 + i)[d]
-            coarse[m] = coarse[m] + t[i * el : (i + 1) * el]
-
-    for c in range(4):
-        p = (c // 2) * n + c % 2
-        add(2, c, pair_update(n, 2, gather(f_ref, n, 2, p), None, mats["tz"][...], w_low, (zpen,)))
+    for m in range(cubed):
+        for x in range(lx):
+            acc[m, x * ly : (x + 1) * ly] = src[m, x].astype(F32)
+    for batch in batches(pairs, ZBATCH):
+        for p, t in zip(batch, sweep(n, 2, f_ref, batch, None, [mat("tz")], w, (zpen,))):
+            for k in range(n):
+                acc[p * n + k] += t[k * el : (k + 1) * el]
 
     finish(fine)
-    half = (n * n) // 2
-    for d, lo, hi, glo, ghi in ((0, r_lo0, r_hi0, g0lo, g0hi), (1, r_lo1, r_hi1, g1lo, g1hi)):
-        glo[...] = lo[...]
-        ghi[...] = hi[...]
-        nb = dot(mats[f"q{d}"][...], jnp.concatenate([pen_b, lo[half], hi[half]], axis=0))
+    low = [(c // 2) * n + c % 2 for c in range(4)]
+    corner = [(m >> 2) * pairs + ((m >> 1) & 1) * n + (m & 1) for m in range(8)]
+    coarse = [acc[m] for m in corner]
+    xpen = None
+    xmats = [mat("t00"), mat("t01")]
+    for d, lo, hi in ((0, r_lo0, r_hi0), (1, r_lo1, r_hi1)):
+        nb = dot(mat(f"q{d}"), jnp.concatenate([pen_b, lo[half], hi[half]], axis=0))
         dp = (jnp.maximum(pen, nb[:el]), jnp.maximum(pen, nb[el:]))
-        pens[2 * d] = dp[0]
-        pens[2 * d + 1] = dp[1]
-        for c in range(4):
-            p = (c // 2) * n + c % 2
-            add(d, c, pair_update(n, d, gather(f_ref, n, d, p), [lo[p // 2], hi[p // 2]],
-                                  mats[f"t{d}{p % 2}"][...], w_low, dp))
+        if d == 0:
+            xpen = dp
+        else:
+            pens[0] = dp[0]
+            pens[1] = dp[1]
+        tm = [mat(f"t{d}0"), mat(f"t{d}1")]
+        for c, t in enumerate(sweep(n, d, f_ref, low, (lo, hi), tm, w_low, dp)):
+            a, b = c // 2, c % 2
+            for i in range(2):
+                m = (i * 4 + a * 2 + b, a * 4 + i * 2 + b)[d]
+                coarse[m] = coarse[m] + t[i * el : (i + 1) * el]
 
     first = [coarse[m] * scale[m] for m in range(8)]
     w0, w1 = math.sqrt(0.5), math.sqrt(1.5)
@@ -322,13 +328,20 @@
             _, _, tr, tl, g = traces(d, c)
             stacked[d, c] = split(tl) + split(tr) + split(g)
         for h in range(2):
-            t = dot(mats[f"c{d}"][...], jnp.concatenate(stacked[d, 2 * h] + stacked[d, 2 * h + 1], axis=0))
+            t = dot(mat(f"c{d}"), jnp.concatenate(stacked[d, 2 * h] + stacked[d, 2 * h + 1], axis=0))
             up[h] = t[:el].astype(BF)
             dn[h] = t[el:].astype(BF)
         if d == 1:
             start_y(ccop)
         else:
             start_x(ccop, cr_lo0, cr_hi0)
+
+    for batch in batches(pairs, XBATCH):
+        for p, t in zip(batch, sweep(n, 0, f_ref, batch, (r_lo0, r_hi0), xmats, w, xpen)):
+            for i in range(n):
+                acc[p + pairs * i] += t[i * el : (i + 1) * el]
+    g1lo[...] = r_lo1[...]
+    g1hi[...] = r_hi1[...]
 
     applied = [3.0 * ((m >> 2) + ((m >> 1) & 1) + (m & 1)) * first[m] for m in range(8)]
 
@@ -345,7 +358,7 @@
     for d, lo, hi in ((0, cr_lo0, cr_hi0), (1, cr_lo1, cr_hi1)):
         for c in range(4):
             m0, m1, tr, tl, g = traces(d, c)
-            t = dot(mats[f"s{d}{c % 2}"][...],
+            t = dot(mat(f"s{d}{c % 2}"),
                     jnp.concatenate(stacked[d, c] + [lo[c // 2], hi[c // 2]], axis=0))
             ju = tr - t[:el]
             jd = t[2 * el : 3 * el] - tl
@@ -356,105 +369,106 @@
         second[m] = first[m] + scale[m] * (coarse[m] - SCALING * applied[m])
 
 
-def fine_kernel(n, names, src, f_ref, g0lo, g0hi, g1lo, g1hi, pens, second, deg, *refs):
-    count = len(names)
-    mats = dict(zip(names, refs[:count]))
-    updated, residual, acc, masks = refs[count:]
-    lx, ly = src.shape[1], src.shape[2]
+def fine_kernel(n, slots, f_ref, acc, g1lo, g1hi, pens, second, deg, packed, updated, residual,
+                ubuf, rbuf, usem, rsem):
+    def mat(name):
+        off, rows, cols = slots[name]
+        return packed[off : off + rows, :cols]
+
+    lx, ly = ubuf.shape[1], ubuf.shape[2]
     el = lx * ly
-    degree = deg[...]
-    for lv in range(n):
-        masks[lv] = jnp.where(degree >= lv, 1.0, 0.0)
-    pairs = n * n
-    w = mats["w"][...]
-
-    def sweep(d, lo, hi):
-        dp = (pens[2 * d], pens[2 * d + 1])
-
-        def one(p, par, q):
-            t = pair_update(n, d, gather(f_ref, n, d, p), [lo[q], hi[q]], mats[f"t{d}{par}"][...], w, dp)
-            base, step = rows_of(n, d, p)
-            for i in range(n):
-                part = t[i * el : (i + 1) * el]
-                if d == 0:
-                    acc[base + step * i] = part
-                else:
-                    acc[base + step * i] += part
-
-        def body(q, carry):
-            one(2 * q, 0, q)
-            one(2 * q + 1, 1, q)
-            return carry
-
-        lax.fori_loop(0, pairs // 2, body, 0, unroll=2)
-        one(pairs - 1, 0, pairs // 2)
-
-    sweep(0, g0lo, g0hi)
-    sweep(1, g1lo, g1hi)
-    zpen = (pens[4],)
-
-    def body(p, carry):
-        field = gather(f_ref, n, 2, p)
-        t = pair_update(n, 2, field, None, mats["tz"][...], w, zpen)
-        top = jnp.maximum(p // n, p % n)
-        for k in range(n):
-            m = p * n + k
-            s = jnp.concatenate([src[m, x] for x in range(lx)], axis=0).astype(F32)
-            r = masks[jnp.maximum(top, k)] * (s + acc[m] + t[k * el : (k + 1) * el])
-            v = field[k].astype(F32)
-            for x in range(lx):
-                residual[m, x] = r[x * ly : (x + 1) * ly].astype(BF)
-                updated[m, x] = v[x * ly : (x + 1) * ly]
-        return carry
-
-    lax.fori_loop(0, pairs, body, 0, unroll=2)
-    for c in range(8):
-        m = (c >> 2) * n * n + ((c >> 1) & 1) * n + (c & 1)
-        v = f_ref[m].astype(F32) + second[c]
+    cubed, pairs = n * n * n, n * n
+    degree = jnp.concatenate([deg[x] for x in range(lx)], axis=0)
+    masks = {lv: jnp.where(degree >= lv, 1.0, 0.0) for lv in range(3, n)}
+    corner = {(m >> 2) * pairs + ((m >> 1) & 1) * n + (m & 1): m for m in range(8)}
+    out_u = pltpu.make_async_copy(ubuf, updated, usem)
+    for m in range(cubed):
+        v = f_ref[m].astype(F32)
+        if m in corner:
+            v = v + second[corner[m]]
         for x in range(lx):
-            updated[m, x] = v[x * ly : (x + 1) * ly]
+            ubuf[m, x] = v[x * ly : (x + 1) * ly]
+    out_u.start()
+    tm = [mat("t10"), mat("t11")]
+    dp = (pens[0], pens[1])
+    out_r = []
+    for batch in batches(pairs, YBATCH):
+        for p, t in zip(batch, sweep(n, 1, f_ref, batch, (g1lo, g1hi), tm, mat("w"), dp)):
+            i, k = p // n, p % n
+            for j in range(n):
+                m = i * pairs + j * n + k
+                r = acc[m] + t[j * el : (j + 1) * el]
+                top = max(i, j, k)
+                if top > 2:
+                    r = masks[top] * r
+                r = r.astype(BF)
+                for x in range(lx):
+                    rbuf[m, x] = r[x * ly : (x + 1) * ly]
+            if k == n - 1:
+                part = pl.ds(i * pairs, pairs)
+                out_r.append(pltpu.make_async_copy(rbuf.at[part], residual.at[part], rsem.at[i]))
+                out_r[-1].start()
+    for c in out_r:
+        c.wait()
+    out_u.wait()
+
+
+ZBATCH = 49
+XBATCH = 49
+YBATCH = 49
+
+
+def pack(mats):
+    slots, parts, off = {}, [], 0
+    for name in sorted(mats):
+        m = mats[name]
+        slots[name] = (off, m.shape[0], m.shape[1])
+        rows = -(-m.shape[0] // 16) * 16
+        parts.append(np.pad(m, ((0, rows - m.shape[0]), (0, 256 - m.shape[1]))))
+        off += rows
+    return slots, np.concatenate(parts)
 
 
 def per_device(solution, source, degree):
     n = solution.shape[0]
     lx, ly, ez = solution.shape[3:]
     el, cubed, half = lx * ly, n * n * n, (n * n) // 2 + 1
-    mats = matrices(n, lx, ly)
+    slots, packed = pack(matrices(n, lx, ly))
+    packed = jnp.asarray(packed)
     single = [0.0 + 2.0 * 12.0 * 0.5, 3.0 + 2.0 * (12.0 * 1.5 - 1.5)]
     scale = [
         0.5 / (SCALING * (single[m >> 2] + single[(m >> 1) & 1] + single[m & 1])) for m in range(8)
     ]
     sol = solution.reshape(cubed, lx, ly, ez)
     src = source.reshape(cubed, lx, ly, ez)
-    deg = degree.reshape(el, ez)
-    srcc = source[:2, :2, :2].reshape(8, el, ez)
     vmem = pl.BlockSpec(memory_space=pltpu.VMEM)
-    names = sorted(mats)
+    hbm = pl.BlockSpec(memory_space=pl.ANY)
     sd = jax.ShapeDtypeStruct
     ghost = (half, el, ez)
     small = (2, el, ez)
     outs = pl.pallas_call(
-        functools.partial(exchange_kernel, n, names, scale),
-        out_shape=[sd((cubed, el, ez), BF)] + [sd(ghost, BF)] * 4 + [sd((6, el, ez), F32), sd((8, el, ez), F32)],
-        in_specs=[vmem] * (3 + len(names)),
-        out_specs=[vmem] * 7,
+        functools.partial(exchange_kernel, n, slots, scale),
+        out_shape=[sd((cubed, el, ez), BF), sd((cubed, el, ez), F32), sd(ghost, BF), sd(ghost, BF),
+                   sd((2, el, ez), F32), sd((8, el, ez), F32)],
+        in_specs=[vmem] * 4,
+        out_specs=[vmem] * 6,
         scratch_shapes=[pltpu.VMEM(ghost, BF)] * 8 + [pltpu.VMEM(small, BF)] * 8
         + [pltpu.SemaphoreType.DMA((8,)), pltpu.SemaphoreType.DMA((8,))],
         compiler_params=pltpu.CompilerParams(
-            collective_id=0, has_side_effects=True, vmem_limit_bytes=40 << 20
+            collective_id=0, has_side_effects=True, vmem_limit_bytes=34 << 20
         ),
         name="exchange",
-    )(sol, deg, srcc, *[jnp.asarray(mats[k]) for k in names])
-    fnames = ["t00", "t01", "t10", "t11", "tz", "w"]
+    )(sol, src, degree, packed)
     updated, residual = pl.pallas_call(
-        functools.partial(fine_kernel, n, fnames),
+        functools.partial(fine_kernel, n, slots),
         out_shape=[sd((cubed, lx, ly, ez), F32), sd((cubed, lx, ly, ez), BF)],
-        in_specs=[vmem] * (9 + len(fnames)),
-        out_specs=[vmem] * 2,
-        scratch_shapes=[pltpu.VMEM((cubed, el, ez), F32), pltpu.VMEM((n, el, ez), F32)],
-        compiler_params=pltpu.CompilerParams(vmem_limit_bytes=48 << 20),
+        in_specs=[vmem] * 8,
+        out_specs=[hbm] * 2,
+        scratch_shapes=[pltpu.VMEM((cubed, lx, ly, ez), F32), pltpu.VMEM((cubed, lx, ly, ez), BF),
+                        pltpu.SemaphoreType.DMA, pltpu.SemaphoreType.DMA((n,))],
+        compiler_params=pltpu.CompilerParams(vmem_limit_bytes=34 << 20),
         name="fine",
-    )(src, *outs, deg, *[jnp.asarray(mats[k]) for k in fnames])
+    )(*outs, degree, packed)
     return updated.reshape(solution.shape), residual.reshape(solution.shape)
 
 

time: 69.2 us -> 29.8 us (0.43); the launches traced: 67.9 us -> 29.5 us
  Pallas kernels: 49 us -> 23.5 us
  local copies, waits for them, and re-layouts: 18.2 us -> 5.32 us
    pallas_call x2, Pallas kernels: 49 us -> 23.5 us  [the longest x1 18.9 us: per_device(): pl.pallas_call(functools.partial(exchange_kernel, n, slots, scale), out_s...]
    unnamed x54 -> x8, local copies, waits for them, and re-layouts: 16.4 us -> 5.32 us
    reshape x2 -> x0, local copies, waits for them, and re-layouts: 0.9 us -> none  [the longest x1 0.88 us: per_device(): deg = degree.reshape(el, ez)]
    slice x1 -> x0, local copies, waits for them, and re-layouts: 0.86 us -> none  [per_device(): srcc = source[:2, :2, :2].reshape(8, el, ez)]
where the time goes in v1:
time: 29.8 us; the launch traced here: 29.5 us
  Pallas kernels  23.5 us (79%)
  local copies, waits for them, and re-layouts  5.32 us (18%)
  between operations  0.65 us (2%)
    pallas_call x1, Pallas kernels, per_device(): pl.pallas_call(functools.partial(exchange_kernel, n, slots, scale), out_s...  18.9 us
    unnamed x8, local copies, waits for them, and re-layouts  5.32 us
    pallas_call x1, Pallas kernels, per_device(): pl.pallas_call(functools.partial(fine_kernel, n, slots), out_shape=[sd((c...  4.65 us

profile of v1, /device:TPU:0, one launch (start us, length us, event | category | flops | bytes accessed | tf_op | source)
XLA Modules:
  0.0 29.5 jit_solution(12630056114107872730)
XLA Ops:
  0.6 0.0 copy-start
  0.6 1.8 %copy-done = bf16[7,7,7,4,4,256]{5,4,3,2,1,0:T(4,128)(2,1)S(1)} copy-done((bf16[7,7,7,4,4,256]{5,4,3,2,1,0:T(4,128)(2,1)S(1)}, bf16[7,7,7,4,4,256]{5,4,3,2,1,0:T(4,128)(2,1)}, u32[]{:S(2)}) %copy-start) | copy-done | bytes 2809880
  2.4 0.0 copy-start.1
  2.4 1.8 %copy-done.1 = bf16[7,7,7,4,4,256]{5,4,3,2,1,0:T(4,128)(2,1)S(1)} copy-done((bf16[7,7,7,4,4,256]{5,4,3,2,1,0:T(4,128)(2,1)S(1)}, bf16[7,7,7,4,4,256]{5,4,3,2,1,0:T(4,128)(2,1)}, u32[]{:S(2)}) %copy-start.1) | copy-done | bytes 2809880
  4.2 0.0 copy-start.2
  4.2 1.0 %copy-done.2 = bf16[944,256]{1,0:T(8,128)(2,1)S(1)} copy-done((bf16[944,256]{1,0:T(8,128)(2,1)S(1)}, bf16[944,256]{1,0:T(8,128)(2,1)}, u32[]{:S(2)}) %copy-start.2) | copy-done | bytes 483352
  5.2 0.0 copy-start.3
  5.2 0.7 %copy-done.3 = s32[4,4,256]{2,1,0:T(4,128)S(1)} copy-done((s32[4,4,256]{2,1,0:T(4,128)S(1)}, s32[4,4,256]{2,1,0:T(4,128)}, u32[]{:S(2)}) %copy-start.3) | copy-done | bytes 16408
  6.0 18.9 %exchange.1 = (bf16[343,16,256]{2,1,0:T(8,128)(2,1)S(1)}, f32[343,16,256]{2,1,0:T(8,128)S(1)}, bf16[25,16,256]{2,1,0:T(8,128)(2,1)S(1)}, bf16[25,16,256]{2,1,0:T...) custom-call(bf16[343,4,4,256]{3,2,1,0:T(4,128)(2,1)S(1)} %bitcast.4, ...), custom_call_target="tpu_custom_call" | custom-call | tf_op jit(solution)/shard_map/exchange/pallas_call | solution.py:449
  24.8 4.6 %fine.1 = (f32[343,4,4,256]{3,2,1,0:T(4,128)}, bf16[343,4,4,256]{3,2,1,0:T(4,128)(2,1)}) custom-call(bf16[343,16,256]{2,1,0:T(8,128)(2,1)S(1)} %get-tuple-element.10.f_ref, f32[343,16,256]{2,1,0:T(8,128)S(1)} %get-tuple-element.11.acc, bf16[25,16,256]{2,1,0:T(8,128)(2,1)S(1)} %get-tuple-element.12.g1lo, bf16[25,16,256]{2,1,0:T(8,128)(2,1)S(1)} %get-tuple-element.13.g1hi, ...), custom_call_target="tpu_custom_call" | custom-call | tf_op jit(solution)/shard_map/fine/pallas_call | solution.py:462
Async XLA Ops:
  0.6 1.8 %copy-start = (bf16[7,7,7,4,4,256]{5,4,3,2,1,0:T(4,128)(2,1)S(1)}, bf16[7,7,7,4,4,256]{5,4,3,2,1,0:T(4,128)(2,1)}, u32[]{:S(2)}) copy-start(bf16[7,7,7,4,4,256]{5,4,3,2,1,0:T(4,128)(2,1)} %param.4) | copy-start | bytes 8429572
  2.4 1.8 %copy-start.1 = (bf16[7,7,7,4,4,256]{5,4,3,2,1,0:T(4,128)(2,1)S(1)}, bf16[7,7,7,4,4,256]{5,4,3,2,1,0:T(4,128)(2,1)}, u32[]{:S(2)}) copy-start(bf16[7,7,7,4,4,256]{5,4,3,2,1,0:T(4,128)(2,1)} %param.5) | copy-start | bytes 8429572
  4.2 1.0 %copy-start.2 = (bf16[944,256]{1,0:T(8,128)(2,1)S(1)}, bf16[944,256]{1,0:T(8,128)(2,1)}, u32[]{:S(2)}) copy-start(bf16[944,256]{1,0:T(8,128)(2,1)} %constant.2.clone.packed) | copy-start | bytes 1449988
  5.2 0.7 %copy-start.3 = (s32[4,4,256]{2,1,0:T(4,128)S(1)}, s32[4,4,256]{2,1,0:T(4,128)}, u32[]{:S(2)}) copy-start(s32[4,4,256]{2,1,0:T(4,128)} %deg.3) | copy-start | bytes 49156

commit v2 on v1

--- a/solution.py
+++ b/solution.py
@@ -174,9 +174,10 @@
     return [list(range(a, min(a + size, total))) for a in range(0, total, size)]
 
 
-def exchange_kernel(n, slots, scale, sol, src, deg, packed, f_ref, acc, g1lo, g1hi, pens, second,
+def exchange_kernel(n, slots, scale, sol_h, src_h, deg_h, packed_h, f_ref, acc_h, g1lo, g1hi, pens, second,
                     s_up0, s_dn0, s_up1, s_dn1, r_lo0, r_hi0, r_lo1, r_hi1,
-                    cs_up0, cs_dn0, cs_up1, cs_dn1, cr_lo0, cr_hi0, cr_lo1, cr_hi1, send, recv):
+                    cs_up0, cs_dn0, cs_up1, cs_dn1, cr_lo0, cr_hi0, cr_lo1, cr_hi1, send, recv,
+                    sol, src, deg, packed, s_ref, acc, asem, isem):
     def mat(name):
         off, rows, cols = slots[name]
         return packed[off : off + rows, :cols]
@@ -188,9 +189,17 @@
     south = {"grp": lax.rem(grp + ngrp - 1, ngrp), "mem": mem}
     north = {"grp": lax.rem(grp + 1, ngrp), "mem": mem}
     has_lo, has_hi = mem > 0, mem < nmem - 1
-    lx, ly = sol.shape[1], sol.shape[2]
+    lx, ly = sol_h.shape[1], sol_h.shape[2]
     el = lx * ly
     cubed, pairs, half = n * n * n, n * n, (n * n) // 2
+
+    loads = [pltpu.make_async_copy(deg_h, deg, isem.at[0]), pltpu.make_async_copy(packed_h, packed, isem.at[1])]
+    for i in range(n):
+        part = pl.ds(i * pairs, pairs)
+        loads.append(pltpu.make_async_copy(sol_h.at[part], sol.at[part], isem.at[2 + i]))
+    loads.append(pltpu.make_async_copy(src_h, src, isem.at[2 + n]))
+    for c in [loads[0]] + loads[2 : 2 + n] + [loads[1], loads[2 + n]]:
+        c.start()
 
     barrier = pltpu.get_barrier_semaphore()
 
@@ -205,9 +214,12 @@
     pl.semaphore_signal(barrier, inc=1, device_id=south, device_id_type=MESH)
     pl.semaphore_signal(barrier, inc=1, device_id=north, device_id_type=MESH)
 
+    loads[0].wait()
     degree = jnp.concatenate([deg[x] for x in range(lx)], axis=0)
     masks = {lv: jnp.where(degree >= lv, 1.0, 0.0).astype(BF) for lv in range(3, n)}
     for m in range(cubed):
+        if m % pairs == 0:
+            loads[2 + m // pairs].wait()
         f_ref[m] = jnp.concatenate([sol[m, x] for x in range(lx)], axis=0)
     for m in range(cubed):
         top = max(m // pairs, (m // n) % n, m % n)
@@ -272,6 +284,7 @@
             c[3].wait_send()
             c[2].wait_recv()
 
+    loads[1].wait()
     fine = copies(0, s_up0, s_dn0, s_up1, s_dn1, r_lo0, r_hi0, r_lo1, r_hi1)
     edges(1, s_up1, s_dn1)
     pl.semaphore_wait(barrier, 2 + has_lo.astype(jnp.int32) + has_hi.astype(jnp.int32))
@@ -282,13 +295,13 @@
     w = mat("w")
     w_low = w[: 2 * el]
     zpen = jnp.maximum(pen, roll(pen, -1))
+    loads[2 + n].wait()
     for m in range(cubed):
-        for x in range(lx):
-            acc[m, x * ly : (x + 1) * ly] = src[m, x].astype(F32)
+        s_ref[m] = jnp.concatenate([src[m, x] for x in range(lx)], axis=0)
     for batch in batches(pairs, ZBATCH):
         for p, t in zip(batch, sweep(n, 2, f_ref, batch, None, [mat("tz")], w, (zpen,))):
             for k in range(n):
-                acc[p * n + k] += t[k * el : (k + 1) * el]
+                acc[p * n + k] = s_ref[p * n + k].astype(F32) + t[k * el : (k + 1) * el]
 
     finish(fine)
     low = [(c // 2) * n + c % 2 for c in range(4)]
@@ -340,6 +353,8 @@
         for p, t in zip(batch, sweep(n, 0, f_ref, batch, (r_lo0, r_hi0), xmats, w, xpen)):
             for i in range(n):
                 acc[p + pairs * i] += t[i * el : (i + 1) * el]
+    acc_out = pltpu.make_async_copy(acc, acc_h, asem)
+    acc_out.start()
     g1lo[...] = r_lo1[...]
     g1hi[...] = r_hi1[...]
 
@@ -367,10 +382,11 @@
             lift(m0, m1, fu, fd, ju, jd)
     for m in range(8):
         second[m] = first[m] + scale[m] * (coarse[m] - SCALING * applied[m])
-
-
-def fine_kernel(n, slots, f_ref, acc, g1lo, g1hi, pens, second, deg, packed, updated, residual,
-                ubuf, rbuf, usem, rsem):
+    acc_out.wait()
+
+
+def fine_kernel(n, slots, f_ref, acc_h, g1lo, g1hi, pens, second, deg, packed, updated, residual,
+                ubuf, rbuf, acc, usem, rsem, asem):
     def mat(name):
         off, rows, cols = slots[name]
         return packed[off : off + rows, :cols]
@@ -381,20 +397,31 @@
     degree = jnp.concatenate([deg[x] for x in range(lx)], axis=0)
     masks = {lv: jnp.where(degree >= lv, 1.0, 0.0) for lv in range(3, n)}
     corner = {(m >> 2) * pairs + ((m >> 1) & 1) * n + (m & 1): m for m in range(8)}
-    out_u = pltpu.make_async_copy(ubuf, updated, usem)
+    loads = []
+    for i in range(n):
+        part = pl.ds(i * pairs, pairs)
+        loads.append(pltpu.make_async_copy(acc_h.at[part], acc.at[part], asem.at[i]))
+        loads[-1].start()
+    out_u = []
     for m in range(cubed):
         v = f_ref[m].astype(F32)
         if m in corner:
             v = v + second[corner[m]]
         for x in range(lx):
             ubuf[m, x] = v[x * ly : (x + 1) * ly]
-    out_u.start()
+        if m % pairs == pairs - 1:
+            i = m // pairs
+            part = pl.ds(i * pairs, pairs)
+            out_u.append(pltpu.make_async_copy(ubuf.at[part], updated.at[part], usem.at[i]))
+            out_u[-1].start()
     tm = [mat("t10"), mat("t11")]
     dp = (pens[0], pens[1])
     out_r = []
     for batch in batches(pairs, YBATCH):
         for p, t in zip(batch, sweep(n, 1, f_ref, batch, (g1lo, g1hi), tm, mat("w"), dp)):
             i, k = p // n, p % n
+            if k == 0:
+                loads[i].wait()
             for j in range(n):
                 m = i * pairs + j * n + k
                 r = acc[m] + t[j * el : (j + 1) * el]
@@ -408,9 +435,8 @@
                 part = pl.ds(i * pairs, pairs)
                 out_r.append(pltpu.make_async_copy(rbuf.at[part], residual.at[part], rsem.at[i]))
                 out_r[-1].start()
-    for c in out_r:
+    for c in out_u + out_r:
         c.wait()
-    out_u.wait()
 
 
 ZBATCH = 49
@@ -450,23 +476,28 @@
         functools.partial(exchange_kernel, n, slots, scale),
         out_shape=[sd((cubed, el, ez), BF), sd((cubed, el, ez), F32), sd(ghost, BF), sd(ghost, BF),
                    sd((2, el, ez), F32), sd((8, el, ez), F32)],
-        in_specs=[vmem] * 4,
-        out_specs=[vmem] * 6,
+        in_specs=[pl.BlockSpec(memory_space=pltpu.HBM)] * 4,
+        out_specs=[vmem, hbm] + [vmem] * 4,
         scratch_shapes=[pltpu.VMEM(ghost, BF)] * 8 + [pltpu.VMEM(small, BF)] * 8
-        + [pltpu.SemaphoreType.DMA((8,)), pltpu.SemaphoreType.DMA((8,))],
+        + [pltpu.SemaphoreType.DMA((8,)), pltpu.SemaphoreType.DMA((8,))]
+        + [pltpu.VMEM((cubed, lx, ly, ez), BF), pltpu.VMEM((cubed, lx, ly, ez), BF),
+           pltpu.VMEM((lx, ly, ez), jnp.int32), pltpu.VMEM(packed.shape, BF),
+           pltpu.VMEM((cubed, el, ez), BF), pltpu.VMEM((cubed, el, ez), F32),
+           pltpu.SemaphoreType.DMA, pltpu.SemaphoreType.DMA((n + 3,))],
         compiler_params=pltpu.CompilerParams(
-            collective_id=0, has_side_effects=True, vmem_limit_bytes=34 << 20
+            collective_id=0, has_side_effects=True, vmem_limit_bytes=48 << 20
         ),
         name="exchange",
     )(sol, src, degree, packed)
     updated, residual = pl.pallas_call(
         functools.partial(fine_kernel, n, slots),
         out_shape=[sd((cubed, lx, ly, ez), F32), sd((cubed, lx, ly, ez), BF)],
-        in_specs=[vmem] * 8,
+        in_specs=[vmem, hbm] + [vmem] * 6,
         out_specs=[hbm] * 2,
         scratch_shapes=[pltpu.VMEM((cubed, lx, ly, ez), F32), pltpu.VMEM((cubed, lx, ly, ez), BF),
-                        pltpu.SemaphoreType.DMA, pltpu.SemaphoreType.DMA((n,))],
-        compiler_params=pltpu.CompilerParams(vmem_limit_bytes=34 << 20),
+                        pltpu.VMEM((cubed, el, ez), F32), pltpu.SemaphoreType.DMA((n,)),
+                        pltpu.SemaphoreType.DMA((n,)), pltpu.SemaphoreType.DMA((n,))],
+        compiler_params=pltpu.CompilerParams(vmem_limit_bytes=48 << 20),
         name="fine",
     )(*outs, degree, packed)
     return updated.reshape(solution.shape), residual.reshape(solution.shape)

time: 29.8 us -> 30.4 us (1.020)
  Pallas kernels: 23.5 us -> 27.8 us
  local copies, waits for them, and re-layouts: 5.32 us -> 1.74 us
    unnamed x8 -> x4, local copies, waits for them, and re-layouts: 5.32 us -> 1.74 us
    pallas_call x1, Pallas kernels: 4.65 us -> 7.45 us  [per_device(): pl.pallas_call(functools.partial(fine_kernel, n, slots), out_shape=[sd((c...]
    pallas_call x1, Pallas kernels: 18.9 us -> 20.3 us  [per_device(): pl.pallas_call(functools.partial(exchange_kernel, n, slots, scale), out_s...]
where the time goes in v2:
time: 30.4 us; the launch traced here: 30.2 us
  Pallas kernels  27.8 us (91%)
  local copies, waits for them, and re-layouts  1.74 us (6%)
  between operations  0.65 us (2%)
    pallas_call x1, Pallas kernels, per_device(): pl.pallas_call(functools.partial(exchange_kernel, n, slots, scale), out_s...  20.3 us
    pallas_call x1, Pallas kernels, per_device(): pl.pallas_call(functools.partial(fine_kernel, n, slots), out_shape=[sd((c...  7.45 us
    unnamed x4, local copies, waits for them, and re-layouts  1.74 us

profile of v2, /device:TPU:0, one launch (start us, length us, event | category | flops | bytes accessed | tf_op | source)
XLA Modules:
  0.0 30.2 jit_solution(10834071904387090345)
XLA Ops:
  0.6 0.0 copy-start
  0.6 1.0 %copy-done = bf16[944,256]{1,0:T(8,128)(2,1)S(1)} copy-done((bf16[944,256]{1,0:T(8,128)(2,1)S(1)}, bf16[944,256]{1,0:T(8,128)(2,1)}, u32[]{:S(2)}) %copy-start) | copy-done | bytes 483352
  1.7 0.0 copy-start.1
  1.7 0.7 %copy-done.1 = s32[4,4,256]{2,1,0:T(4,128)S(1)} copy-done((s32[4,4,256]{2,1,0:T(4,128)S(1)}, s32[4,4,256]{2,1,0:T(4,128)}, u32[]{:S(2)}) %copy-start.1) | copy-done | bytes 16408
  2.4 20.3 %exchange.1 = (bf16[343,16,256]{2,1,0:T(8,128)(2,1)S(1)}, f32[343,16,256]{2,1,0:T(8,128)}, bf16[25,16,256]{2,1,0:T(8,128)(2,1)S(1)}, bf16[25,16,256]{2,1,0:T(8,1...) custom-call(bf16[343,4,4,256]{3,2,1,0:T(4,128)(2,1)} %bitcast.4, bf16[343,4,4,256]{3,2,1,0:T(4,128)(2,1)} %bitcast.5, ...), custom_call_target="tpu_custom_call" | custom-call | tf_op jit(solution)/shard_map/exchange/pallas_call | solution.py:475
  22.7 7.5 %fine.1 = (f32[343,4,4,256]{3,2,1,0:T(4,128)}, bf16[343,4,4,256]{3,2,1,0:T(4,128)(2,1)}) custom-call(bf16[343,16,256]{2,1,0:T(8,128)(2,1)S(1)} %get-tuple-element.10.f_ref, f32[343,16,256]{2,1,0:T(8,128)} %get-tuple-element.11.acc_h, bf16[25,16,256]{2,1,0:T(8,128)(2,1)S(1)} %get-tuple-element.12.g1lo, bf16[25,16,256]{2,1,0:T(8,128)(2,1)S(1)} %get-tuple-element.13.g1hi, ...), custom_call_target="tpu_custom_call" | custom-call | tf_op jit(solution)/shard_map/fine/pallas_call | solution.py:492
Async XLA Ops:
  0.6 1.0 %copy-start = (bf16[944,256]{1,0:T(8,128)(2,1)S(1)}, bf16[944,256]{1,0:T(8,128)(2,1)}, u32[]{:S(2)}) copy-start(bf16[944,256]{1,0:T(8,128)(2,1)} %constant.2.clone.packed_h.packed) | copy-start | bytes 1449988
  1.7 0.7 %copy-start.1 = (s32[4,4,256]{2,1,0:T(4,128)S(1)}, s32[4,4,256]{2,1,0:T(4,128)}, u32[]{:S(2)}) copy-start(s32[4,4,256]{2,1,0:T(4,128)} %deg.1) | copy-start | bytes 49156
